TPU v7x, 512 devices: a whole 4x8x8 slice. The times are simulated.
512 devices in a mesh: theta: 32 (over x_lo, z, core), gz: 16 (over y, x_hi).
Axes of the slice: x: 4 (x_hi: 2, x_lo: 2; x = x_hi * 2 + x_lo), y: 8, z: 8, core: 2. Of those that a mesh axis runs over, the one named last changes fastest.
Arguments:
- velocity: float32 [3, 256, 256, 256], P(None, 'theta', 'gz'), may hold values from -6 to 6
- adjoint_seed: float32 [3, 256, 256, 256], P(None, 'theta', 'gz'), may hold values from -6 to 6
- rotor_offset: int32 [2], replicated, may hold values from 0 to 255
- design_mask: int32 [256, 256, 256], P('theta', 'gz'), may hold values 0 or 1
- interface_band_weight: bfloat16 [256, 8], replicated, may hold values from -0.375 to 0.375
Outputs:
- ending_velocity: float32 [3, 256, 256, 256], P(None, 'theta', 'gz')
- adjoint_field: float32 [3, 256, 256, 256], P(None, 'theta', 'gz')
All inputs are finite; a program needn't handle non-finite values. No bound on the sum of `design_mask` on one device may be relied on, other than what follows from the above.
Results may differ from a plain program's by a relative error of at most 0.00076.
Values sent between devices are 32-bit elements; how exact they have to be, the bound alone decides.
No kernel may reach another device: no remote copies, remote signals or barrier semaphores. Data moves between devices by JAX's collectives and lax.ppermute only.
A program may use at most 64 MiB of HBM per device.

v0:
```python
import jax
import jax.numpy as jnp
from jax import lax
from jax.sharding import PartitionSpec as P

NR = 256
RB = 128
BAND = 8
STEPS = 2


def shifted(x, axis, by):
    peers = lax.axis_size(axis)
    return lax.ppermute(x, axis, [(i, (i + by) % peers) for i in range(peers)])


def padded(block, sides, width, periodic):
    for axis, dim in sides:
        count = lax.axis_size(axis)
        forward = [(i, i + 1) for i in range(count - 1)]
        if periodic:
            forward.append((count - 1, 0))
        backward = [(target, source) for source, target in forward]
        low = lax.ppermute(
            lax.slice_in_dim(block, block.shape[dim] - width, None, axis=dim), axis, forward
        )
        high = lax.ppermute(lax.slice_in_dim(block, 0, width, axis=dim), axis, backward)
        block = jnp.concatenate([low, block, high], axis=dim)
    return block


def rotate(flow_field, shift):
    sector_count = lax.axis_size("theta")
    width = flow_field.shape[1]
    total = width * sector_count
    shift = jnp.mod(shift, total)
    blocks = shift // width
    remain = shift % width
    rotor = flow_field[..., :RB]
    levels = sector_count.bit_length() - 1
    for level in range(levels):
        moved = shifted(rotor, "theta", 1 << level)
        rotor = jnp.where(blocks >> level & 1 == 1, moved, rotor)
    before = shifted(rotor, "theta", 1)
    combined_parts = jnp.concatenate([before, rotor], axis=1)
    start = width - remain
    rotor = lax.dynamic_slice_in_dim(combined_parts, start, width, axis=1)
    return jnp.concatenate([rotor, flow_field[..., RB:]], axis=3)


def neighbours(flow_field):
    beside_all = padded(flow_field, (("theta", 1),), 1, True)
    sliced_layers = padded(flow_field, (("gz", 2),), 1, False)
    radial = jnp.pad(flow_field, ((0, 0), (0, 0), (0, 0), (1, 1)))
    return (
        beside_all[:, 2:],
        beside_all[:, :-2],
        sliced_layers[:, :, 2:],
        sliced_layers[:, :, :-2],
        radial[..., 2:],
        radial[..., :-2],
    )


def body(velocity, adjoint_seed, rotor_offset, design_mask, interface_band_weight):
    lower = RB - BAND // 2
    upper = RB + BAND // 2
    shape = velocity.shape
    solid = design_mask.astype(jnp.float32)
    flow_field = velocity
    viscosity_values = []
    for step in range(STEPS):
        moved = rotate(flow_field, rotor_offset[step])
        flat = moved.astype(jnp.bfloat16).reshape(-1, NR)
        mix = jnp.dot(flat, interface_band_weight, preferred_element_type=jnp.float32)
        mixed = moved.at[..., lower:upper].add(mix.reshape(shape[0], shape[1], shape[2], BAND))
        tp, tm, zp, zm, rp, rm = neighbours(mixed)
        strain_rate = jnp.sum(
            ((tp - tm) * 0.5) ** 2 + ((zp - zm) * 0.5) ** 2 + ((rp - rm) * 0.5) ** 2, axis=0
        )
        visc = 0.05 + 0.95 * (1.0 + 4.0 * strain_rate) ** (-0.25)
        viscosity_values.append(visc)
        laplace = tp + tm + zp + zm + rp + rm - 6.0 * mixed
        flow_field = mixed + 0.1 * visc * laplace - 0.5 * solid * mixed
    adjoint = adjoint_seed
    for step in range(STEPS - 1, -1, -1):
        scaled = viscosity_values[step] * adjoint
        tp, tm, zp, zm, rp, rm = neighbours(scaled)
        laplace = tp + tm + zp + zm + rp + rm - 6.0 * scaled
        after = adjoint + 0.1 * laplace - 0.5 * solid * adjoint
        band = after[..., lower:upper].astype(jnp.bfloat16).reshape(-1, BAND)
        back = jnp.dot(band, interface_band_weight.T, preferred_element_type=jnp.float32)
        after = after + back.reshape(shape)
        adjoint = rotate(after, -rotor_offset[step])
    return (flow_field, adjoint)


def solution(mesh):
    return jax.shard_map(
        body,
        mesh=mesh,
        in_specs=(
            P(None, "theta", "gz", None),
            P(None, "theta", "gz", None),
            P(),
            P("theta", "gz", None),
            P(),
        ),
        out_specs=(P(None, "theta", "gz", None), P(None, "theta", "gz", None)),
        check_vma=False,
    )
```

profile of v0, /device:TPU:28, one launch (start us, length us, event | category | flops | bytes accessed | tf_op | source)
XLA Modules:
  0.0 345.2 jit_solution(14299572217153007055)
XLA Ops:
  6.9 9.1 %collective-permute-done = f32[3,8,16,128]{3,2,1,0:T(8,128)S(1)} collective-permute-done((f32[3,8,16,128]{3,2,1,0:T(8,128)S(1)}, f32[3,8,16,128]{3,2,1,0:T(8,128)S(1)}, u32[]{:S(2)}, u32[]{:S(2)}) %collective-permute-start) | collective-permute-done | bytes 196640 | tf_op jit(solution)/shard_map/ppermute | solution.py:14
  18.0 7.7 %collective-permute-done.1 = f32[3,8,16,128]{3,2,1,0:T(8,128)S(1)} collective-permute-done((f32[3,8,16,128]{3,2,1,0:T(8,128)S(1)}, f32[3,8,16,128]{3,2,1,0:T(8,128)S(1)}, u32[]{:S(2)}, u32[]{:S(2)}) %collective-permute-start.1) | collective-permute-done | bytes 196640 | tf_op jit(solution)/shard_map/ppermute | solution.py:14
  27.7 9.0 %collective-permute-done.2 = f32[3,8,16,128]{3,2,1,0:T(8,128)S(1)} collective-permute-done((f32[3,8,16,128]{3,2,1,0:T(8,128)S(1)}, f32[3,8,16,128]{3,2,1,0:T(8,128)S(1)}, u32[]{:S(2)}, u32[]{:S(2)}) %collective-permute-start.2) | collective-permute-done | bytes 196640 | tf_op jit(solution)/shard_map/ppermute | solution.py:14
  36.7 5.4 %collective-permute-start.3 = (f32[3,8,16,128]{3,2,1,0:T(8,128)S(1)}, f32[3,8,16,128]{3,2,1,0:T(8,128)S(1)}, u32[]{:S(2)}, u32[]{:S(2)}) collective-permute-start(f32[3,8,16,128]{3,2,1,0:T(8,128)S(1)} %broadcast_select_fusion.12), channel_id=1, source_target_pairs={{0,128},{16,144},{32,160},{48,176},{64,192},{80,208},{96,224},{112... | collective-permute-start | bytes 589832 | tf_op jit(solution)/shard_map/ppermute | solution.py:14
  42.1 10.1 %collective-permute-done.3 = f32[3,8,16,128]{3,2,1,0:T(8,128)S(1)} collective-permute-done((f32[3,8,16,128]{3,2,1,0:T(8,128)S(1)}, f32[3,8,16,128]{3,2,1,0:T(8,128)S(1)}, u32[]{:S(2)}, u32[]{:S(2)}) %collective-permute-start.3) | collective-permute-done | bytes 196640 | tf_op jit(solution)/shard_map/ppermute | solution.py:14
  55.3 5.0 %collective-permute-done.4 = f32[3,8,16,128]{3,2,1,0:T(8,128)S(1)} collective-permute-done((f32[3,8,16,128]{3,2,1,0:T(8,128)S(1)}, f32[3,8,16,128]{3,2,1,0:T(8,128)S(1)}, u32[]{:S(2)}, u32[]{:S(2)}) %collective-permute-start.4) | collective-permute-done | bytes 196640 | tf_op jit(solution)/shard_map/ppermute | solution.py:14
  62.3 7.2 %collective-permute-done.5 = f32[3,8,16,128]{3,2,1,0:T(8,128)S(1)} collective-permute-done((f32[3,8,16,128]{3,2,1,0:T(8,128)S(1)}, f32[3,8,16,128]{3,2,1,0:T(8,128)S(1)}, u32[]{:S(2)}, u32[]{:S(2)}) %collective-permute-start.5) | collective-permute-done | bytes 196640 | tf_op jit(solution)/shard_map/ppermute | solution.py:14
  76.1 7.0 %collective-permute-start.9 = (f32[3,8,1,256]{3,2,1,0:T(1,128)S(1)}, f32[3,8,1,256]{3,2,1,0:T(1,128)S(1)}, u32[]{:S(2)}, u32[]{:S(2)}) collective-permute-start(f32[3,8,1,256]{3,2,1,0:T(1,128)S(1)} %get-tuple-element.46), channel_id=1, source_target_pairs={{0,1},{1,2},{2,3},{3,4},{4,5},{5,6},{6,7},{7,8},{8,9},{9,10},{10,1... | collective-permute-start | bytes 73736 | tf_op jit(solution)/shard_map/ppermute | solution.py:24
  87.5 5.0 %collective-permute-done.7 = f32[3,1,16,256]{3,2,1,0:T(8,128)S(1)} collective-permute-done((f32[3,1,16,256]{3,2,1,0:T(8,128)S(1)}, f32[3,1,16,256]{3,2,1,0:T(8,128)S(1)}, u32[]{:S(2)}, u32[]{:S(2)}) %collective-permute-start.7) | collective-permute-done | bytes 49184 | tf_op jit(solution)/shard_map/ppermute | solution.py:24
  97.2 5.2 %collective-permute-done.10 = f32[3,8,16,128]{3,2,1,0:T(8,128)S(1)} collective-permute-done((f32[3,8,16,128]{3,2,1,0:T(8,128)S(1)}, f32[3,8,16,128]{3,2,1,0:T(8,128)S(1)}, u32[]{:S(2)}, u32[]{:S(2)}) %collective-permute-start.10) | collective-permute-done | bytes 196640 | tf_op jit(solution)/shard_map/ppermute | solution.py:14
  104.4 8.5 %collective-permute-done.11 = f32[3,8,16,128]{3,2,1,0:T(8,128)S(1)} collective-permute-done((f32[3,8,16,128]{3,2,1,0:T(8,128)S(1)}, f32[3,8,16,128]{3,2,1,0:T(8,128)S(1)}, u32[]{:S(2)}, u32[]{:S(2)}) %collective-permute-start.11) | collective-permute-done | bytes 196640 | tf_op jit(solution)/shard_map/ppermute | solution.py:14
  114.9 9.7 %collective-permute-done.12 = f32[3,8,16,128]{3,2,1,0:T(8,128)S(1)} collective-permute-done((f32[3,8,16,128]{3,2,1,0:T(8,128)S(1)}, f32[3,8,16,128]{3,2,1,0:T(8,128)S(1)}, u32[]{:S(2)}, u32[]{:S(2)}) %collective-permute-start.12) | collective-permute-done | bytes 196640 | tf_op jit(solution)/shard_map/ppermute | solution.py:14
  126.5 11.9 %collective-permute-done.13 = f32[3,8,16,128]{3,2,1,0:T(8,128)S(1)} collective-permute-done((f32[3,8,16,128]{3,2,1,0:T(8,128)S(1)}, f32[3,8,16,128]{3,2,1,0:T(8,128)S(1)}, u32[]{:S(2)}, u32[]{:S(2)}) %collective-permute-start.13) | collective-permute-done | bytes 196640 | tf_op jit(solution)/shard_map/ppermute | solution.py:14
  140.5 5.5 %collective-permute-done.14 = f32[3,8,16,128]{3,2,1,0:T(8,128)S(1)} collective-permute-done((f32[3,8,16,128]{3,2,1,0:T(8,128)S(1)}, f32[3,8,16,128]{3,2,1,0:T(8,128)S(1)}, u32[]{:S(2)}, u32[]{:S(2)}) %collective-permute-start.14) | collective-permute-done | bytes 196640 | tf_op jit(solution)/shard_map/ppermute | solution.py:14
  148.0 7.2 %collective-permute-done.15 = f32[3,8,16,128]{3,2,1,0:T(8,128)S(1)} collective-permute-done((f32[3,8,16,128]{3,2,1,0:T(8,128)S(1)}, f32[3,8,16,128]{3,2,1,0:T(8,128)S(1)}, u32[]{:S(2)}, u32[]{:S(2)}) %collective-permute-start.15) | collective-permute-done | bytes 196640 | tf_op jit(solution)/shard_map/ppermute | solution.py:14
  165.6 7.7 %collective-permute-start.19 = (f32[3,8,1,256]{3,2,1,0:T(1,128)S(1)}, f32[3,8,1,256]{3,2,1,0:T(1,128)S(1)}, u32[]{:S(2)}, u32[]{:S(2)}) collective-permute-start(f32[3,8,1,256]{3,2,1,0:T(1,128)S(1)} %get-tuple-element.40), channel_id=1, source_target_pairs={{0,1},{1,2},{2,3},{3,4},{4,5},{5,6},{6,7},{7,8},{8,9},{9,10},{10,1... | collective-permute-start | bytes 73736 | tf_op jit(solution)/shard_map/ppermute | solution.py:24
  177.2 5.8 %collective-permute-start.20 = (f32[3,1,16,256]{3,2,1,0:T(8,128)S(1)}, f32[3,1,16,256]{3,2,1,0:T(8,128)S(1)}, u32[]{:S(2)}, u32[]{:S(2)}) collective-permute-start(f32[3,1,16,256]{3,2,1,0:T(8,128)S(1)} %get-tuple-element.34), channel_id=1, source_target_pairs={{16,0},{32,16},{48,32},{64,48},{80,64},{96,80},{112,96},{128,112},... | collective-permute-start | bytes 147464 | tf_op jit(solution)/shard_map/ppermute | solution.py:27
  183.0 7.8 %collective-permute-start.23 = (f32[3,8,1,256]{3,2,1,0:T(1,128)S(1)}, f32[3,8,1,256]{3,2,1,0:T(1,128)S(1)}, u32[]{:S(2)}, u32[]{:S(2)}) collective-permute-start(f32[3,8,1,256]{3,2,1,0:T(1,128)S(1)} %get-tuple-element.37), channel_id=1, source_target_pairs={{0,1},{1,2},{2,3},{3,4},{4,5},{5,6},{6,7},{7,8},{8,9},{9,10},{10,1... | collective-permute-start | bytes 73736 | tf_op jit(solution)/shard_map/ppermute | solution.py:24
  192.7 7.4 %collective-permute-done.22 = f32[3,8,1,256]{3,2,1,0:T(1,128)S(1)} collective-permute-done((f32[3,8,1,256]{3,2,1,0:T(1,128)S(1)}, f32[3,8,1,256]{3,2,1,0:T(1,128)S(1)}, u32[]{:S(2)}, u32[]{:S(2)}) %collective-permute-start.22) | collective-permute-done | bytes 24608 | tf_op jit(solution)/shard_map/ppermute | solution.py:27
  203.4 6.5 %collective-permute-done.24 = f32[3,8,16,128]{3,2,1,0:T(8,128)S(1)} collective-permute-done((f32[3,8,16,128]{3,2,1,0:T(8,128)S(1)}, f32[3,8,16,128]{3,2,1,0:T(8,128)S(1)}, u32[]{:S(2)}, u32[]{:S(2)}) %collective-permute-start.24) | collective-permute-done | bytes 196640 | tf_op jit(solution)/shard_map/ppermute | solution.py:14
  211.9 8.5 %collective-permute-done.25 = f32[3,8,16,128]{3,2,1,0:T(8,128)S(1)} collective-permute-done((f32[3,8,16,128]{3,2,1,0:T(8,128)S(1)}, f32[3,8,16,128]{3,2,1,0:T(8,128)S(1)}, u32[]{:S(2)}, u32[]{:S(2)}) %collective-permute-start.25) | collective-permute-done | bytes 196640 | tf_op jit(solution)/shard_map/ppermute | solution.py:14
  222.4 8.6 %collective-permute-done.26 = f32[3,8,16,128]{3,2,1,0:T(8,128)S(1)} collective-permute-done((f32[3,8,16,128]{3,2,1,0:T(8,128)S(1)}, f32[3,8,16,128]{3,2,1,0:T(8,128)S(1)}, u32[]{:S(2)}, u32[]{:S(2)}) %collective-permute-start.26) | collective-permute-done | bytes 196640 | tf_op jit(solution)/shard_map/ppermute | solution.py:14
  233.0 11.1 %collective-permute-done.27 = f32[3,8,16,128]{3,2,1,0:T(8,128)S(1)} collective-permute-done((f32[3,8,16,128]{3,2,1,0:T(8,128)S(1)}, f32[3,8,16,128]{3,2,1,0:T(8,128)S(1)}, u32[]{:S(2)}, u32[]{:S(2)}) %collective-permute-start.27) | collective-permute-done | bytes 196640 | tf_op jit(solution)/shard_map/ppermute | solution.py:14
  254.3 7.2 %collective-permute-done.29 = f32[3,8,16,128]{3,2,1,0:T(8,128)S(1)} collective-permute-done((f32[3,8,16,128]{3,2,1,0:T(8,128)S(1)}, f32[3,8,16,128]{3,2,1,0:T(8,128)S(1)}, u32[]{:S(2)}, u32[]{:S(2)}) %collective-permute-start.29) | collective-permute-done | bytes 196640 | tf_op jit(solution)/shard_map/ppermute | solution.py:14
  263.5 5.8 %collective-permute-start.30 = (f32[3,1,16,256]{3,2,1,0:T(8,128)S(1)}, f32[3,1,16,256]{3,2,1,0:T(8,128)S(1)}, u32[]{:S(2)}, u32[]{:S(2)}) collective-permute-start(f32[3,1,16,256]{3,2,1,0:T(8,128)S(1)} %get-tuple-element.28), channel_id=1, source_target_pairs={{16,0},{32,16},{48,32},{64,48},{80,64},{96,80},{112,96},{128,112},... | collective-permute-start | bytes 147464 | tf_op jit(solution)/shard_map/ppermute | solution.py:27
  271.4 5.2 %collective-permute-start.32 = (f32[3,8,1,256]{3,2,1,0:T(1,128)S(1)}, f32[3,8,1,256]{3,2,1,0:T(1,128)S(1)}, u32[]{:S(2)}, u32[]{:S(2)}) collective-permute-start(f32[3,8,1,256]{3,2,1,0:T(1,128)S(1)} %get-tuple-element.30), channel_id=1, source_target_pairs={{1,0},{2,1},{3,2},{4,3},{5,4},{6,5},{7,6},{8,7},{9,8},{10,9},{11,1... | collective-permute-start | bytes 73736 | tf_op jit(solution)/shard_map/ppermute | solution.py:27
  284.1 6.5 %collective-permute-done.34 = f32[3,8,16,128]{3,2,1,0:T(8,128)S(1)} collective-permute-done((f32[3,8,16,128]{3,2,1,0:T(8,128)S(1)}, f32[3,8,16,128]{3,2,1,0:T(8,128)S(1)}, u32[]{:S(2)}, u32[]{:S(2)}) %collective-permute-start.34) | collective-permute-done | bytes 196640 | tf_op jit(solution)/shard_map/ppermute | solution.py:14
  292.5 8.5 %collective-permute-done.35 = f32[3,8,16,128]{3,2,1,0:T(8,128)S(1)} collective-permute-done((f32[3,8,16,128]{3,2,1,0:T(8,128)S(1)}, f32[3,8,16,128]{3,2,1,0:T(8,128)S(1)}, u32[]{:S(2)}, u32[]{:S(2)}) %collective-permute-start.35) | collective-permute-done | bytes 196640 | tf_op jit(solution)/shard_map/ppermute | solution.py:14
  303.0 10.3 %collective-permute-done.36 = f32[3,8,16,128]{3,2,1,0:T(8,128)S(1)} collective-permute-done((f32[3,8,16,128]{3,2,1,0:T(8,128)S(1)}, f32[3,8,16,128]{3,2,1,0:T(8,128)S(1)}, u32[]{:S(2)}, u32[]{:S(2)}) %collective-permute-start.36) | collective-permute-done | bytes 196640 | tf_op jit(solution)/shard_map/ppermute | solution.py:14
  315.2 12.5 %collective-permute-done.37 = f32[3,8,16,128]{3,2,1,0:T(8,128)S(1)} collective-permute-done((f32[3,8,16,128]{3,2,1,0:T(8,128)S(1)}, f32[3,8,16,128]{3,2,1,0:T(8,128)S(1)}, u32[]{:S(2)}, u32[]{:S(2)}) %collective-permute-start.37) | collective-permute-done | bytes 196640 | tf_op jit(solution)/shard_map/ppermute | solution.py:14
  329.7 5.6 %collective-permute-done.38 = f32[3,8,16,128]{3,2,1,0:T(8,128)S(1)} collective-permute-done((f32[3,8,16,128]{3,2,1,0:T(8,128)S(1)}, f32[3,8,16,128]{3,2,1,0:T(8,128)S(1)}, u32[]{:S(2)}, u32[]{:S(2)}) %collective-permute-start.38) | collective-permute-done | bytes 196640 | tf_op jit(solution)/shard_map/ppermute | solution.py:14
  338.3 6.1 %collective-permute-done.39 = f32[3,8,16,128]{3,2,1,0:T(8,128)S(1)} collective-permute-done((f32[3,8,16,128]{3,2,1,0:T(8,128)S(1)}, f32[3,8,16,128]{3,2,1,0:T(8,128)S(1)}, u32[]{:S(2)}, u32[]{:S(2)}) %collective-permute-start.39) | collective-permute-done | bytes 196640 | tf_op jit(solution)/shard_map/ppermute | solution.py:14
  (113 shorter events, 94.1 us)
Async XLA Ops:
  1.7 14.4 %collective-permute-start = (f32[3,8,16,128]{3,2,1,0:T(8,128)S(1)}, f32[3,8,16,128]{3,2,1,0:T(8,128)S(1)}, u32[]{:S(2)}, u32[]{:S(2)}) collective-permute-start(f32[3,8,16,128]{3,2,1,0:T(8,128)S(1)} %slice.236), channel_id=1, source_target_pairs={{0,16},{16,32},{32,48},{48,64},{64,80},{80,96},{96,112},{112,128},... | collective-permute-start | bytes 589832 | tf_op jit(solution)/shard_map/ppermute | solution.py:14
  16.1 9.7 %collective-permute-start.1 = (f32[3,8,16,128]{3,2,1,0:T(8,128)S(1)}, f32[3,8,16,128]{3,2,1,0:T(8,128)S(1)}, u32[]{:S(2)}, u32[]{:S(2)}) collective-permute-start(f32[3,8,16,128]{3,2,1,0:T(8,128)S(1)} %get-tuple-element.48), channel_id=1, source_target_pairs={{0,32},{16,48},{32,64},{48,80},{64,96},{80,112},{96,128},{112,144}... | collective-permute-start | bytes 589832 | tf_op jit(solution)/shard_map/ppermute | solution.py:14
  25.8 10.9 %collective-permute-start.2 = (f32[3,8,16,128]{3,2,1,0:T(8,128)S(1)}, f32[3,8,16,128]{3,2,1,0:T(8,128)S(1)}, u32[]{:S(2)}, u32[]{:S(2)}) collective-permute-start(f32[3,8,16,128]{3,2,1,0:T(8,128)S(1)} %broadcast_select_fusion.11), channel_id=1, source_target_pairs={{0,64},{16,80},{32,96},{48,112},{64,128},{80,144},{96,160},{112,17... | collective-permute-start | bytes 589832 | tf_op jit(solution)/shard_map/ppermute | solution.py:14
  36.7 15.5 %collective-permute-start.3 = (f32[3,8,16,128]{3,2,1,0:T(8,128)S(1)}, f32[3,8,16,128]{3,2,1,0:T(8,128)S(1)}, u32[]{:S(2)}, u32[]{:S(2)}) collective-permute-start(f32[3,8,16,128]{3,2,1,0:T(8,128)S(1)} %broadcast_select_fusion.12), channel_id=1, source_target_pairs={{0,128},{16,144},{32,160},{48,176},{64,192},{80,208},{96,224},{112... | collective-permute-start | bytes 589832 | tf_op jit(solution)/shard_map/ppermute | solution.py:14
  60.3 9.1 %collective-permute-start.5 = (f32[3,8,16,128]{3,2,1,0:T(8,128)S(1)}, f32[3,8,16,128]{3,2,1,0:T(8,128)S(1)}, u32[]{:S(2)}, u32[]{:S(2)}) collective-permute-start(f32[3,8,16,128]{3,2,1,0:T(8,128)S(1)} %broadcast_select_fusion.14), channel_id=1, source_target_pairs={{0,16},{16,32},{32,48},{48,64},{64,80},{80,96},{96,112},{112,128},... | collective-permute-start | bytes 589832 | tf_op jit(solution)/shard_map/ppermute | solution.py:14
  73.6 13.8 %collective-permute-start.8 = (f32[3,8,1,256]{3,2,1,0:T(1,128)S(1)}, f32[3,8,1,256]{3,2,1,0:T(1,128)S(1)}, u32[]{:S(2)}, u32[]{:S(2)}) collective-permute-start(f32[3,8,1,256]{3,2,1,0:T(1,128)S(1)} %get-tuple-element.47), channel_id=1, source_target_pairs={{1,0},{2,1},{3,2},{4,3},{5,4},{6,5},{7,6},{8,7},{9,8},{10,9},{11,1... | collective-permute-start | bytes 73736 | tf_op jit(solution)/shard_map/ppermute | solution.py:27
  76.1 11.4 %collective-permute-start.9 = (f32[3,8,1,256]{3,2,1,0:T(1,128)S(1)}, f32[3,8,1,256]{3,2,1,0:T(1,128)S(1)}, u32[]{:S(2)}, u32[]{:S(2)}) collective-permute-start(f32[3,8,1,256]{3,2,1,0:T(1,128)S(1)} %get-tuple-element.46), channel_id=1, source_target_pairs={{0,1},{1,2},{2,3},{3,4},{4,5},{5,6},{6,7},{7,8},{8,9},{9,10},{10,1... | collective-permute-start | bytes 73736 | tf_op jit(solution)/shard_map/ppermute | solution.py:24
  93.3 9.1 %collective-permute-start.10 = (f32[3,8,16,128]{3,2,1,0:T(8,128)S(1)}, f32[3,8,16,128]{3,2,1,0:T(8,128)S(1)}, u32[]{:S(2)}, u32[]{:S(2)}) collective-permute-start(f32[3,8,16,128]{3,2,1,0:T(8,128)S(1)} %slice.294), channel_id=1, source_target_pairs={{0,16},{16,32},{32,48},{48,64},{64,80},{80,96},{96,112},{112,128},... | collective-permute-start | bytes 589832 | tf_op jit(solution)/shard_map/ppermute | solution.py:14
  102.5 10.4 %collective-permute-start.11 = (f32[3,8,16,128]{3,2,1,0:T(8,128)S(1)}, f32[3,8,16,128]{3,2,1,0:T(8,128)S(1)}, u32[]{:S(2)}, u32[]{:S(2)}) collective-permute-start(f32[3,8,16,128]{3,2,1,0:T(8,128)S(1)} %get-tuple-element.42), channel_id=1, source_target_pairs={{0,32},{16,48},{32,64},{48,80},{64,96},{80,112},{96,128},{112,144}... | collective-permute-start | bytes 589832 | tf_op jit(solution)/shard_map/ppermute | solution.py:14
  112.9 11.6 %collective-permute-start.12 = (f32[3,8,16,128]{3,2,1,0:T(8,128)S(1)}, f32[3,8,16,128]{3,2,1,0:T(8,128)S(1)}, u32[]{:S(2)}, u32[]{:S(2)}) collective-permute-start(f32[3,8,16,128]{3,2,1,0:T(8,128)S(1)} %broadcast_select_fusion.16), channel_id=1, source_target_pairs={{0,64},{16,80},{32,96},{48,112},{64,128},{80,144},{96,160},{112,17... | collective-permute-start | bytes 589832 | tf_op jit(solution)/shard_map/ppermute | solution.py:14
  124.6 13.9 %collective-permute-start.13 = (f32[3,8,16,128]{3,2,1,0:T(8,128)S(1)}, f32[3,8,16,128]{3,2,1,0:T(8,128)S(1)}, u32[]{:S(2)}, u32[]{:S(2)}) collective-permute-start(f32[3,8,16,128]{3,2,1,0:T(8,128)S(1)} %broadcast_select_fusion.17), channel_id=1, source_target_pairs={{0,128},{16,144},{32,160},{48,176},{64,192},{80,208},{96,224},{112... | collective-permute-start | bytes 589832 | tf_op jit(solution)/shard_map/ppermute | solution.py:14
  146.0 9.1 %collective-permute-start.15 = (f32[3,8,16,128]{3,2,1,0:T(8,128)S(1)}, f32[3,8,16,128]{3,2,1,0:T(8,128)S(1)}, u32[]{:S(2)}, u32[]{:S(2)}) collective-permute-start(f32[3,8,16,128]{3,2,1,0:T(8,128)S(1)} %broadcast_select_fusion.19), channel_id=1, source_target_pairs={{0,16},{16,32},{32,48},{48,64},{64,80},{80,96},{96,112},{112,128},... | collective-permute-start | bytes 589832 | tf_op jit(solution)/shard_map/ppermute | solution.py:14
  159.2 15.5 %collective-permute-start.16 = (f32[3,1,16,256]{3,2,1,0:T(8,128)S(1)}, f32[3,1,16,256]{3,2,1,0:T(8,128)S(1)}, u32[]{:S(2)}, u32[]{:S(2)}) collective-permute-start(f32[3,1,16,256]{3,2,1,0:T(8,128)S(1)} %get-tuple-element.39), channel_id=1, source_target_pairs={{16,0},{32,16},{48,32},{64,48},{80,64},{96,80},{112,96},{128,112},... | collective-permute-start | bytes 147464 | tf_op jit(solution)/shard_map/ppermute | solution.py:27
  161.2 13.6 %collective-permute-start.17 = (f32[3,1,16,256]{3,2,1,0:T(8,128)S(1)}, f32[3,1,16,256]{3,2,1,0:T(8,128)S(1)}, u32[]{:S(2)}, u32[]{:S(2)}) collective-permute-start(f32[3,1,16,256]{3,2,1,0:T(8,128)S(1)} %get-tuple-element.38), channel_id=1, source_target_pairs={{0,16},{16,32},{32,48},{48,64},{64,80},{80,96},{96,112},{112,128},... | collective-permute-start | bytes 147464 | tf_op jit(solution)/shard_map/ppermute | solution.py:24
  163.6 9.6 %collective-permute-start.18 = (f32[3,8,1,256]{3,2,1,0:T(1,128)S(1)}, f32[3,8,1,256]{3,2,1,0:T(1,128)S(1)}, u32[]{:S(2)}, u32[]{:S(2)}) collective-permute-start(f32[3,8,1,256]{3,2,1,0:T(1,128)S(1)} %get-tuple-element.41), channel_id=1, source_target_pairs={{1,0},{2,1},{3,2},{4,3},{5,4},{6,5},{7,6},{8,7},{9,8},{10,9},{11,1... | collective-permute-start | bytes 73736 | tf_op jit(solution)/shard_map/ppermute | solution.py:27
  165.6 9.2 %collective-permute-start.19 = (f32[3,8,1,256]{3,2,1,0:T(1,128)S(1)}, f32[3,8,1,256]{3,2,1,0:T(1,128)S(1)}, u32[]{:S(2)}, u32[]{:S(2)}) collective-permute-start(f32[3,8,1,256]{3,2,1,0:T(1,128)S(1)} %get-tuple-element.40), channel_id=1, source_target_pairs={{0,1},{1,2},{2,3},{3,4},{4,5},{5,6},{6,7},{7,8},{8,9},{9,10},{10,1... | collective-permute-start | bytes 73736 | tf_op jit(solution)/shard_map/ppermute | solution.py:24
  175.2 24.9 %collective-permute-start.21 = (f32[3,1,16,256]{3,2,1,0:T(8,128)S(1)}, f32[3,1,16,256]{3,2,1,0:T(8,128)S(1)}, u32[]{:S(2)}, u32[]{:S(2)}) collective-permute-start(f32[3,1,16,256]{3,2,1,0:T(8,128)S(1)} %get-tuple-element.35), channel_id=1, source_target_pairs={{0,16},{16,32},{32,48},{48,64},{64,80},{80,96},{96,112},{112,128},... | collective-permute-start | bytes 147464 | tf_op jit(solution)/shard_map/ppermute | solution.py:24
  177.2 23.0 %collective-permute-start.20 = (f32[3,1,16,256]{3,2,1,0:T(8,128)S(1)}, f32[3,1,16,256]{3,2,1,0:T(8,128)S(1)}, u32[]{:S(2)}, u32[]{:S(2)}) collective-permute-start(f32[3,1,16,256]{3,2,1,0:T(8,128)S(1)} %get-tuple-element.34), channel_id=1, source_target_pairs={{16,0},{32,16},{48,32},{64,48},{80,64},{96,80},{112,96},{128,112},... | collective-permute-start | bytes 147464 | tf_op jit(solution)/shard_map/ppermute | solution.py:27
  183.0 9.8 %collective-permute-start.23 = (f32[3,8,1,256]{3,2,1,0:T(1,128)S(1)}, f32[3,8,1,256]{3,2,1,0:T(1,128)S(1)}, u32[]{:S(2)}, u32[]{:S(2)}) collective-permute-start(f32[3,8,1,256]{3,2,1,0:T(1,128)S(1)} %get-tuple-element.37), channel_id=1, source_target_pairs={{0,1},{1,2},{2,3},{3,4},{4,5},{5,6},{6,7},{7,8},{8,9},{9,10},{10,1... | collective-permute-start | bytes 73736 | tf_op jit(solution)/shard_map/ppermute | solution.py:24
  190.8 9.3 %collective-permute-start.22 = (f32[3,8,1,256]{3,2,1,0:T(1,128)S(1)}, f32[3,8,1,256]{3,2,1,0:T(1,128)S(1)}, u32[]{:S(2)}, u32[]{:S(2)}) collective-permute-start(f32[3,8,1,256]{3,2,1,0:T(1,128)S(1)} %get-tuple-element.36), channel_id=1, source_target_pairs={{1,0},{2,1},{3,2},{4,3},{5,4},{6,5},{7,6},{8,7},{9,8},{10,9},{11,1... | collective-permute-start | bytes 73736 | tf_op jit(solution)/shard_map/ppermute | solution.py:27
  200.8 9.1 %collective-permute-start.24 = (f32[3,8,16,128]{3,2,1,0:T(8,128)S(1)}, f32[3,8,16,128]{3,2,1,0:T(8,128)S(1)}, u32[]{:S(2)}, u32[]{:S(2)}) collective-permute-start(f32[3,8,16,128]{3,2,1,0:T(8,128)S(1)} %slice.307), channel_id=1, source_target_pairs={{0,16},{16,32},{32,48},{48,64},{64,80},{80,96},{96,112},{112,128},... | collective-permute-start | bytes 589832 | tf_op jit(solution)/shard_map/ppermute | solution.py:14
  210.0 10.4 %collective-permute-start.25 = (f32[3,8,16,128]{3,2,1,0:T(8,128)S(1)}, f32[3,8,16,128]{3,2,1,0:T(8,128)S(1)}, u32[]{:S(2)}, u32[]{:S(2)}) collective-permute-start(f32[3,8,16,128]{3,2,1,0:T(8,128)S(1)} %get-tuple-element.32), channel_id=1, source_target_pairs={{0,32},{16,48},{32,64},{48,80},{64,96},{80,112},{96,128},{112,144}... | collective-permute-start | bytes 589832 | tf_op jit(solution)/shard_map/ppermute | solution.py:14
  220.4 10.6 %collective-permute-start.26 = (f32[3,8,16,128]{3,2,1,0:T(8,128)S(1)}, f32[3,8,16,128]{3,2,1,0:T(8,128)S(1)}, u32[]{:S(2)}, u32[]{:S(2)}) collective-permute-start(f32[3,8,16,128]{3,2,1,0:T(8,128)S(1)} %broadcast_select_fusion.1), channel_id=1, source_target_pairs={{0,64},{16,80},{32,96},{48,112},{64,128},{80,144},{96,160},{112,17... | collective-permute-start | bytes 589832 | tf_op jit(solution)/shard_map/ppermute | solution.py:14
  231.0 13.0 %collective-permute-start.27 = (f32[3,8,16,128]{3,2,1,0:T(8,128)S(1)}, f32[3,8,16,128]{3,2,1,0:T(8,128)S(1)}, u32[]{:S(2)}, u32[]{:S(2)}) collective-permute-start(f32[3,8,16,128]{3,2,1,0:T(8,128)S(1)} %broadcast_select_fusion.2), channel_id=1, source_target_pairs={{0,128},{16,144},{32,160},{48,176},{64,192},{80,208},{96,224},{112... | collective-permute-start | bytes 589832 | tf_op jit(solution)/shard_map/ppermute | solution.py:14
  252.4 9.1 %collective-permute-start.29 = (f32[3,8,16,128]{3,2,1,0:T(8,128)S(1)}, f32[3,8,16,128]{3,2,1,0:T(8,128)S(1)}, u32[]{:S(2)}, u32[]{:S(2)}) collective-permute-start(f32[3,8,16,128]{3,2,1,0:T(8,128)S(1)} %broadcast_select_fusion.4), channel_id=1, source_target_pairs={{0,16},{16,32},{32,48},{48,64},{64,80},{80,96},{96,112},{112,128},... | collective-permute-start | bytes 589832 | tf_op jit(solution)/shard_map/ppermute | solution.py:14
  261.6 19.2 %collective-permute-start.31 = (f32[3,1,16,256]{3,2,1,0:T(8,128)S(1)}, f32[3,1,16,256]{3,2,1,0:T(8,128)S(1)}, u32[]{:S(2)}, u32[]{:S(2)}) collective-permute-start(f32[3,1,16,256]{3,2,1,0:T(8,128)S(1)} %get-tuple-element.29), channel_id=1, source_target_pairs={{0,16},{16,32},{32,48},{48,64},{64,80},{80,96},{96,112},{112,128},... | collective-permute-start | bytes 147464 | tf_op jit(solution)/shard_map/ppermute | solution.py:24
  263.5 17.3 %collective-permute-start.30 = (f32[3,1,16,256]{3,2,1,0:T(8,128)S(1)}, f32[3,1,16,256]{3,2,1,0:T(8,128)S(1)}, u32[]{:S(2)}, u32[]{:S(2)}) collective-permute-start(f32[3,1,16,256]{3,2,1,0:T(8,128)S(1)} %get-tuple-element.28), channel_id=1, source_target_pairs={{16,0},{32,16},{48,32},{64,48},{80,64},{96,80},{112,96},{128,112},... | collective-permute-start | bytes 147464 | tf_op jit(solution)/shard_map/ppermute | solution.py:27
  271.4 9.3 %collective-permute-start.32 = (f32[3,8,1,256]{3,2,1,0:T(1,128)S(1)}, f32[3,8,1,256]{3,2,1,0:T(1,128)S(1)}, u32[]{:S(2)}, u32[]{:S(2)}) collective-permute-start(f32[3,8,1,256]{3,2,1,0:T(1,128)S(1)} %get-tuple-element.30), channel_id=1, source_target_pairs={{1,0},{2,1},{3,2},{4,3},{5,4},{6,5},{7,6},{8,7},{9,8},{10,9},{11,1... | collective-permute-start | bytes 73736 | tf_op jit(solution)/shard_map/ppermute | solution.py:27
  281.5 9.1 %collective-permute-start.34 = (f32[3,8,16,128]{3,2,1,0:T(8,128)S(1)}, f32[3,8,16,128]{3,2,1,0:T(8,128)S(1)}, u32[]{:S(2)}, u32[]{:S(2)}) collective-permute-start(f32[3,8,16,128]{3,2,1,0:T(8,128)S(1)} %slice.314), channel_id=1, source_target_pairs={{0,16},{16,32},{32,48},{48,64},{64,80},{80,96},{96,112},{112,128},... | collective-permute-start | bytes 589832 | tf_op jit(solution)/shard_map/ppermute | solution.py:14
  290.6 10.4 %collective-permute-start.35 = (f32[3,8,16,128]{3,2,1,0:T(8,128)S(1)}, f32[3,8,16,128]{3,2,1,0:T(8,128)S(1)}, u32[]{:S(2)}, u32[]{:S(2)}) collective-permute-start(f32[3,8,16,128]{3,2,1,0:T(8,128)S(1)} %get-tuple-element.26), channel_id=1, source_target_pairs={{0,32},{16,48},{32,64},{48,80},{64,96},{80,112},{96,128},{112,144}... | collective-permute-start | bytes 589832 | tf_op jit(solution)/shard_map/ppermute | solution.py:14
  301.1 12.2 %collective-permute-start.36 = (f32[3,8,16,128]{3,2,1,0:T(8,128)S(1)}, f32[3,8,16,128]{3,2,1,0:T(8,128)S(1)}, u32[]{:S(2)}, u32[]{:S(2)}) collective-permute-start(f32[3,8,16,128]{3,2,1,0:T(8,128)S(1)} %broadcast_select_fusion.6), channel_id=1, source_target_pairs={{0,64},{16,80},{32,96},{48,112},{64,128},{80,144},{96,160},{112,17... | collective-permute-start | bytes 589832 | tf_op jit(solution)/shard_map/ppermute | solution.py:14
  313.3 14.4 %collective-permute-start.37 = (f32[3,8,16,128]{3,2,1,0:T(8,128)S(1)}, f32[3,8,16,128]{3,2,1,0:T(8,128)S(1)}, u32[]{:S(2)}, u32[]{:S(2)}) collective-permute-start(f32[3,8,16,128]{3,2,1,0:T(8,128)S(1)} %broadcast_select_fusion.7), channel_id=1, source_target_pairs={{0,128},{16,144},{32,160},{48,176},{64,192},{80,208},{96,224},{112... | collective-permute-start | bytes 589832 | tf_op jit(solution)/shard_map/ppermute | solution.py:14
  (12 other events, 167.6 us)
where the time goes:
time: 347 us; the launch traced here: 345 us
  waiting for transfers between devices  209 us (60%)
  starting transfers between devices  114 us (33%)
  local copies, waits for them, and re-layouts  10.2 us (3%)
  between operations  6.82 us (2%)
  other arithmetic  4.71 us (1%)
    ppermute x24, waiting for transfers between devices, shifted(): return lax.ppermute(x, axis, [(i, (i + by) % peers) for i in range(peers)])  191 us
    ppermute x24, starting transfers between devices, shifted(): return lax.ppermute(x, axis, [(i, (i + by) % peers) for i in range(peers)])  53.5 us
    ppermute x8, starting transfers between devices, padded(): lax.ppermute(lax.slice_in_dim(block, block.shape[dim] - width, None, axis...  33.2 us
    ppermute x8, starting transfers between devices, padded(): lax.ppermute(lax.slice_in_dim(block, 0, width, axis=dim), axis, backward)  26.9 us
    ppermute x8, waiting for transfers between devices, padded(): lax.ppermute(lax.slice_in_dim(block, 0, width, axis=dim), axis, backward)  11.5 us
    scatter-add x2, local copies, waits for them, and re-layouts, body(): moved.at[..., lower:upper]  7.59 us
  transfers between devices with their start and end apart: 40, of which 28 were waited for; matrix products, arithmetic and copies ran while one was open for 1% of the time, Pallas kernels for 0%

commit v1 on v0

--- a/solution.py
+++ b/solution.py
@@ -32,19 +32,17 @@
 def rotate(flow_field, shift):
     sector_count = lax.axis_size("theta")
     width = flow_field.shape[1]
-    total = width * sector_count
-    shift = jnp.mod(shift, total)
+    shift = jnp.mod(shift, width * sector_count)
     blocks = shift // width
     remain = shift % width
     rotor = flow_field[..., :RB]
-    levels = sector_count.bit_length() - 1
-    for level in range(levels):
-        moved = shifted(rotor, "theta", 1 << level)
-        rotor = jnp.where(blocks >> level & 1 == 1, moved, rotor)
-    before = shifted(rotor, "theta", 1)
-    combined_parts = jnp.concatenate([before, rotor], axis=1)
-    start = width - remain
-    rotor = lax.dynamic_slice_in_dim(combined_parts, start, width, axis=1)
+
+    def moved_by(count):
+        return lambda x: (shifted(x, "theta", count + 1), shifted(x, "theta", count))
+
+    before, here = lax.switch(blocks, [moved_by(b) for b in range(sector_count)], rotor)
+    combined_parts = jnp.concatenate([before, here], axis=1)
+    rotor = lax.dynamic_slice_in_dim(combined_parts, width - remain, width, axis=1)
     return jnp.concatenate([rotor, flow_field[..., RB:]], axis=3)
 
 
@@ -67,13 +65,14 @@
     upper = RB + BAND // 2
     shape = velocity.shape
     solid = design_mask.astype(jnp.float32)
+    spread = jnp.pad(interface_band_weight, ((0, 0), (lower, NR - upper)))
     flow_field = velocity
     viscosity_values = []
     for step in range(STEPS):
         moved = rotate(flow_field, rotor_offset[step])
         flat = moved.astype(jnp.bfloat16).reshape(-1, NR)
-        mix = jnp.dot(flat, interface_band_weight, preferred_element_type=jnp.float32)
-        mixed = moved.at[..., lower:upper].add(mix.reshape(shape[0], shape[1], shape[2], BAND))
+        mix = jnp.dot(flat, spread, preferred_element_type=jnp.float32)
+        mixed = moved + mix.reshape(shape)
         tp, tm, zp, zm, rp, rm = neighbours(mixed)
         strain_rate = jnp.sum(
             ((tp - tm) * 0.5) ** 2 + ((zp - zm) * 0.5) ** 2 + ((rp - rm) * 0.5) ** 2, axis=0

time: 347 us -> 186 us (0.54)
  the two profiles are of different devices: /device:TPU:28 before, /device:TPU:33 now
where the time goes in v1:
time: 186 us; the launch traced here: 185 us
  starting transfers between devices  100 us (54%)
  waiting for transfers between devices  65.6 us (35%)
  other arithmetic  7.7 us (4%)
  between operations  6.5 us (3%)
  local copies, waits for them, and re-layouts  3.44 us (2%)
    ppermute x8, waiting for transfers between devices, shifted(): return lax.ppermute(x, axis, [(i, (i + by) % peers) for i in range(peers)])  55.6 us
    ppermute x8, starting transfers between devices, shifted(): return lax.ppermute(x, axis, [(i, (i + by) % peers) for i in range(peers)])  41.7 us
    ppermute x8, starting transfers between devices, padded(): lax.ppermute(lax.slice_in_dim(block, 0, width, axis=dim), axis, backward)  35.8 us
    ppermute x8, starting transfers between devices, padded(): lax.ppermute(lax.slice_in_dim(block, block.shape[dim] - width, None, axis...  22.6 us
    ppermute x8, waiting for transfers between devices, padded(): lax.ppermute(lax.slice_in_dim(block, block.shape[dim] - width, None, axis...  8.52 us
    concatenate x4, other arithmetic, rotate(): combined_parts = jnp.concatenate([before, here], axis=1)  3.83 us
  transfers between devices with their start and end apart: 24, of which 11 were waited for; matrix products, arithmetic and copies ran while one was open for 0% of the time, Pallas kernels for 0%

profile of v1, /device:TPU:33, one launch (start us, length us, event | category | flops | bytes accessed | tf_op | source)
XLA Modules:
  0.0 184.6 jit_solution(2281726525850961362)
XLA Ops:
  5.9 30.7 %conditional.4 = (f32[3,8,16,128]{3,2,1,0:T(8,128)}, f32[3,8,16,128]{3,2,1,0:T(8,128)}) conditional(s32[]{:T(128)} %clamp.13, f32[3,8,16,128]{3,2,1,0:T(8,128)S(1)} %get-tuple-element.168, f32[3,8,16,128]{3,2,1,0:T(8,128)S(1)} %get-tuple-element.168, f32[3,8,16,128]{3,2,1,0:T(8,128)S(1)} %get-tuple-element.168, ...), branch_computations={%region_0.1_spmd, %region_1.2_spmd, %region_2.3_spmd, %region_3.4_... | conditional | bytes 1572960 | solution.py:43
  5.9 11.2 %collective-permute-start.23 = (f32[3,8,16,128]{3,2,1,0:T(8,128)S(1)}, f32[3,8,16,128]{3,2,1,0:T(8,128)}, u32[]{:S(2)}, u32[]{:S(2)}) collective-permute-start(f32[3,8,16,128]{3,2,1,0:T(8,128)S(1)} %param.11), channel_id=1, source_target_pairs={{0,176},{16,192},{32,208},{48,224},{64,240},{80,256},{96,272},{112... | collective-permute-start | bytes 589832 | tf_op jit(solution)/shard_map/cond/branch_11_fun/ppermute | solution.py:14
  17.1 3.1 %collective-permute-start.22 = (f32[3,8,16,128]{3,2,1,0:T(8,128)S(1)}, f32[3,8,16,128]{3,2,1,0:T(8,128)}, u32[]{:S(2)}, u32[]{:S(2)}) collective-permute-start(f32[3,8,16,128]{3,2,1,0:T(8,128)S(1)} %param.11), channel_id=1, source_target_pairs={{0,192},{16,208},{32,224},{48,240},{64,256},{80,272},{96,288},{112... | collective-permute-start | bytes 589832 | tf_op jit(solution)/shard_map/cond/branch_11_fun/ppermute | solution.py:14
  20.2 7.0 %collective-permute-done.23 = f32[3,8,16,128]{3,2,1,0:T(8,128)} collective-permute-done((f32[3,8,16,128]{3,2,1,0:T(8,128)S(1)}, f32[3,8,16,128]{3,2,1,0:T(8,128)}, u32[]{:S(2)}, u32[]{:S(2)}) %collective-permute-start.23) | collective-permute-done | bytes 196640 | tf_op jit(solution)/shard_map/cond/branch_11_fun/ppermute | solution.py:14
  27.3 9.3 %collective-permute-done.22 = f32[3,8,16,128]{3,2,1,0:T(8,128)} collective-permute-done((f32[3,8,16,128]{3,2,1,0:T(8,128)S(1)}, f32[3,8,16,128]{3,2,1,0:T(8,128)}, u32[]{:S(2)}, u32[]{:S(2)}) %collective-permute-start.22) | collective-permute-done | bytes 196640 | tf_op jit(solution)/shard_map/cond/branch_11_fun/ppermute | solution.py:14
  37.9 4.7 %collective-permute-start.259 = (f32[3,8,1,256]{3,2,1,0:T(1,128)S(1)}, f32[3,8,1,256]{3,2,1,0:T(1,128)S(1)}, u32[]{:S(2)}, u32[]{:S(2)}) collective-permute-start(f32[3,8,1,256]{3,2,1,0:T(1,128)S(1)} %get-tuple-element.166), channel_id=1, source_target_pairs={{0,1},{1,2},{2,3},{3,4},{4,5},{5,6},{6,7},{7,8},{8,9},{9,10},{10,1... | collective-permute-start | bytes 73736 | tf_op jit(solution)/shard_map/ppermute | solution.py:24
  42.6 4.2 %collective-permute-start.258 = (f32[3,8,1,256]{3,2,1,0:T(1,128)S(1)}, f32[3,8,1,256]{3,2,1,0:T(1,128)S(1)}, u32[]{:S(2)}, u32[]{:S(2)}) collective-permute-start(f32[3,8,1,256]{3,2,1,0:T(1,128)S(1)} %get-tuple-element.167), channel_id=1, source_target_pairs={{1,0},{2,1},{3,2},{4,3},{5,4},{6,5},{7,6},{8,7},{9,8},{10,9},{11,1... | collective-permute-start | bytes 73736 | tf_op jit(solution)/shard_map/ppermute | solution.py:27
  48.8 2.9 %collective-permute-start.256 = (f32[3,1,16,256]{3,2,1,0:T(8,128)S(1)}, f32[3,1,16,256]{3,2,1,0:T(8,128)S(1)}, u32[]{:S(2)}, u32[]{:S(2)}) collective-permute-start(f32[3,1,16,256]{3,2,1,0:T(8,128)S(1)} %get-tuple-element.165), channel_id=1, source_target_pairs={{16,0},{32,16},{48,32},{64,48},{80,64},{96,80},{112,96},{128,112},... | collective-permute-start | bytes 147464 | tf_op jit(solution)/shard_map/ppermute | solution.py:27
  55.3 23.6 %conditional.5 = (f32[3,8,16,128]{3,2,1,0:T(8,128)}, f32[3,8,16,128]{3,2,1,0:T(8,128)}) conditional(s32[]{:T(128)} %clamp.12, f32[3,8,16,128]{3,2,1,0:T(8,128)S(1)} %get-tuple-element.162, f32[3,8,16,128]{3,2,1,0:T(8,128)S(1)} %get-tuple-element.162, f32[3,8,16,128]{3,2,1,0:T(8,128)S(1)} %get-tuple-element.162, ...), branch_computations={%region_33.34_spmd, %region_34.35_spmd, %region_35.36_spmd, %regio... | conditional | bytes 1572960 | solution.py:43
  55.3 3.0 %collective-permute-start.103 = (f32[3,8,16,128]{3,2,1,0:T(8,128)S(1)}, f32[3,8,16,128]{3,2,1,0:T(8,128)}, u32[]{:S(2)}, u32[]{:S(2)}) collective-permute-start(f32[3,8,16,128]{3,2,1,0:T(8,128)S(1)} %param.51), channel_id=1, source_target_pairs={{0,304},{16,320},{32,336},{48,352},{64,368},{80,384},{96,400},{112... | collective-permute-start | bytes 589832 | tf_op jit(solution)/shard_map/cond/branch_19_fun/ppermute | solution.py:14
  58.3 8.1 %collective-permute-start.102 = (f32[3,8,16,128]{3,2,1,0:T(8,128)S(1)}, f32[3,8,16,128]{3,2,1,0:T(8,128)}, u32[]{:S(2)}, u32[]{:S(2)}) collective-permute-start(f32[3,8,16,128]{3,2,1,0:T(8,128)S(1)} %param.51), channel_id=1, source_target_pairs={{0,320},{16,336},{32,352},{48,368},{64,384},{80,400},{96,416},{112... | collective-permute-start | bytes 589832 | tf_op jit(solution)/shard_map/cond/branch_19_fun/ppermute | solution.py:14
  66.5 12.4 %collective-permute-done.102 = f32[3,8,16,128]{3,2,1,0:T(8,128)} collective-permute-done((f32[3,8,16,128]{3,2,1,0:T(8,128)S(1)}, f32[3,8,16,128]{3,2,1,0:T(8,128)}, u32[]{:S(2)}, u32[]{:S(2)}) %collective-permute-start.102) | collective-permute-done | bytes 196640 | tf_op jit(solution)/shard_map/cond/branch_19_fun/ppermute | solution.py:14
  82.1 3.0 %collective-permute-start.260 = (f32[3,1,16,256]{3,2,1,0:T(8,128)S(1)}, f32[3,1,16,256]{3,2,1,0:T(8,128)S(1)}, u32[]{:S(2)}, u32[]{:S(2)}) collective-permute-start(f32[3,1,16,256]{3,2,1,0:T(8,128)S(1)} %get-tuple-element.159), channel_id=1, source_target_pairs={{16,0},{32,16},{48,32},{64,48},{80,64},{96,80},{112,96},{128,112},... | collective-permute-start | bytes 147464 | tf_op jit(solution)/shard_map/ppermute | solution.py:27
  85.1 2.4 %collective-permute-start.263 = (f32[3,8,1,256]{3,2,1,0:T(1,128)S(1)}, f32[3,8,1,256]{3,2,1,0:T(1,128)S(1)}, u32[]{:S(2)}, u32[]{:S(2)}) collective-permute-start(f32[3,8,1,256]{3,2,1,0:T(1,128)S(1)} %get-tuple-element.160), channel_id=1, source_target_pairs={{0,1},{1,2},{2,3},{3,4},{4,5},{5,6},{6,7},{7,8},{8,9},{9,10},{10,1... | collective-permute-start | bytes 73736 | tf_op jit(solution)/shard_map/ppermute | solution.py:24
  87.6 6.8 %collective-permute-start.262 = (f32[3,8,1,256]{3,2,1,0:T(1,128)S(1)}, f32[3,8,1,256]{3,2,1,0:T(1,128)S(1)}, u32[]{:S(2)}, u32[]{:S(2)}) collective-permute-start(f32[3,8,1,256]{3,2,1,0:T(1,128)S(1)} %get-tuple-element.161), channel_id=1, source_target_pairs={{1,0},{2,1},{3,2},{4,3},{5,4},{6,5},{7,6},{8,7},{9,8},{10,9},{11,1... | collective-permute-start | bytes 73736 | tf_op jit(solution)/shard_map/ppermute | solution.py:27
  96.7 6.9 %collective-permute-start.264 = (f32[3,1,16,256]{3,2,1,0:T(8,128)S(1)}, f32[3,1,16,256]{3,2,1,0:T(8,128)S(1)}, u32[]{:S(2)}, u32[]{:S(2)}) collective-permute-start(f32[3,1,16,256]{3,2,1,0:T(8,128)S(1)} %get-tuple-element.154), channel_id=1, source_target_pairs={{16,0},{32,16},{48,32},{64,48},{80,64},{96,80},{112,96},{128,112},... | collective-permute-start | bytes 147464 | tf_op jit(solution)/shard_map/ppermute | solution.py:27
  105.5 7.5 %collective-permute-start.266 = (f32[3,8,1,256]{3,2,1,0:T(1,128)S(1)}, f32[3,8,1,256]{3,2,1,0:T(1,128)S(1)}, u32[]{:S(2)}, u32[]{:S(2)}) collective-permute-start(f32[3,8,1,256]{3,2,1,0:T(1,128)S(1)} %get-tuple-element.156), channel_id=1, source_target_pairs={{1,0},{2,1},{3,2},{4,3},{5,4},{6,5},{7,6},{8,7},{9,8},{10,9},{11,1... | collective-permute-start | bytes 73736 | tf_op jit(solution)/shard_map/ppermute | solution.py:27
  115.7 5.5 %collective-permute-done.267 = f32[3,8,1,256]{3,2,1,0:T(1,128)S(1)} collective-permute-done((f32[3,8,1,256]{3,2,1,0:T(1,128)S(1)}, f32[3,8,1,256]{3,2,1,0:T(1,128)S(1)}, u32[]{:S(2)}, u32[]{:S(2)}) %collective-permute-start.267) | collective-permute-done | bytes 24608 | tf_op jit(solution)/shard_map/ppermute | solution.py:24
  121.9 17.6 %conditional.6 = (f32[3,8,16,128]{3,2,1,0:T(8,128)}, f32[3,8,16,128]{3,2,1,0:T(8,128)}) conditional(s32[]{:T(128)} %clamp.15, f32[3,8,16,128]{3,2,1,0:T(8,128)S(1)} %get-tuple-element.152, f32[3,8,16,128]{3,2,1,0:T(8,128)S(1)} %get-tuple-element.152, f32[3,8,16,128]{3,2,1,0:T(8,128)S(1)} %get-tuple-element.152, ...), branch_computations={%region_66.67_spmd, %region_67.68_spmd, %region_68.69_spmd, %regio... | conditional | bytes 1572960 | solution.py:43
  122.0 2.0 %collective-permute-start.155 = (f32[3,8,16,128]{3,2,1,0:T(8,128)S(1)}, f32[3,8,16,128]{3,2,1,0:T(8,128)}, u32[]{:S(2)}, u32[]{:S(2)}) collective-permute-start(f32[3,8,16,128]{3,2,1,0:T(8,128)S(1)} %param.77), channel_id=1, source_target_pairs={{0,208},{16,224},{32,240},{48,256},{64,272},{80,288},{96,304},{112... | collective-permute-start | bytes 589832 | tf_op jit(solution)/shard_map/cond/branch_13_fun/ppermute | solution.py:14
  124.0 6.0 %collective-permute-start.154 = (f32[3,8,16,128]{3,2,1,0:T(8,128)S(1)}, f32[3,8,16,128]{3,2,1,0:T(8,128)}, u32[]{:S(2)}, u32[]{:S(2)}) collective-permute-start(f32[3,8,16,128]{3,2,1,0:T(8,128)S(1)} %param.77), channel_id=1, source_target_pairs={{0,224},{16,240},{32,256},{48,272},{64,288},{80,304},{96,320},{112... | collective-permute-start | bytes 589832 | tf_op jit(solution)/shard_map/cond/branch_13_fun/ppermute | solution.py:14
  130.0 2.1 %collective-permute-done.155 = f32[3,8,16,128]{3,2,1,0:T(8,128)} collective-permute-done((f32[3,8,16,128]{3,2,1,0:T(8,128)S(1)}, f32[3,8,16,128]{3,2,1,0:T(8,128)}, u32[]{:S(2)}, u32[]{:S(2)}) %collective-permute-start.155) | collective-permute-done | bytes 196640 | tf_op jit(solution)/shard_map/cond/branch_13_fun/ppermute | solution.py:14
  132.1 7.4 %collective-permute-done.154 = f32[3,8,16,128]{3,2,1,0:T(8,128)} collective-permute-done((f32[3,8,16,128]{3,2,1,0:T(8,128)S(1)}, f32[3,8,16,128]{3,2,1,0:T(8,128)}, u32[]{:S(2)}, u32[]{:S(2)}) %collective-permute-start.154) | collective-permute-done | bytes 196640 | tf_op jit(solution)/shard_map/cond/branch_13_fun/ppermute | solution.py:14
  140.6 2.6 %collective-permute-start.268 = (f32[3,1,16,256]{3,2,1,0:T(8,128)S(1)}, f32[3,1,16,256]{3,2,1,0:T(8,128)S(1)}, u32[]{:S(2)}, u32[]{:S(2)}) collective-permute-start(f32[3,1,16,256]{3,2,1,0:T(8,128)S(1)} %get-tuple-element.148), channel_id=1, source_target_pairs={{16,0},{32,16},{48,32},{64,48},{80,64},{96,80},{112,96},{128,112},... | collective-permute-start | bytes 147464 | tf_op jit(solution)/shard_map/ppermute | solution.py:27
  143.2 3.0 %collective-permute-start.269 = (f32[3,1,16,256]{3,2,1,0:T(8,128)S(1)}, f32[3,1,16,256]{3,2,1,0:T(8,128)S(1)}, u32[]{:S(2)}, u32[]{:S(2)}) collective-permute-start(f32[3,1,16,256]{3,2,1,0:T(8,128)S(1)} %get-tuple-element.149), channel_id=1, source_target_pairs={{0,16},{16,32},{32,48},{48,64},{64,80},{80,96},{96,112},{112,128},... | collective-permute-start | bytes 147464 | tf_op jit(solution)/shard_map/ppermute | solution.py:24
  148.1 4.9 %collective-permute-start.271 = (f32[3,8,1,256]{3,2,1,0:T(1,128)S(1)}, f32[3,8,1,256]{3,2,1,0:T(1,128)S(1)}, u32[]{:S(2)}, u32[]{:S(2)}) collective-permute-start(f32[3,8,1,256]{3,2,1,0:T(1,128)S(1)} %get-tuple-element.151), channel_id=1, source_target_pairs={{0,1},{1,2},{2,3},{3,4},{4,5},{5,6},{6,7},{7,8},{8,9},{9,10},{10,1... | collective-permute-start | bytes 73736 | tf_op jit(solution)/shard_map/ppermute | solution.py:24
  153.7 3.0 %collective-permute-done.271 = f32[3,8,1,256]{3,2,1,0:T(1,128)S(1)} collective-permute-done((f32[3,8,1,256]{3,2,1,0:T(1,128)S(1)}, f32[3,8,1,256]{3,2,1,0:T(1,128)S(1)}, u32[]{:S(2)}, u32[]{:S(2)}) %collective-permute-start.271) | collective-permute-done | bytes 24608 | tf_op jit(solution)/shard_map/ppermute | solution.py:24
  157.3 25.5 %conditional.7 = (f32[3,8,16,128]{3,2,1,0:T(8,128)}, f32[3,8,16,128]{3,2,1,0:T(8,128)}) conditional(s32[]{:T(128)} %clamp.14, f32[3,8,16,128]{3,2,1,0:T(8,128)S(1)} %get-tuple-element.146, f32[3,8,16,128]{3,2,1,0:T(8,128)S(1)} %get-tuple-element.146, f32[3,8,16,128]{3,2,1,0:T(8,128)S(1)} %get-tuple-element.146, ...), branch_computations={%region_98.99_spmd, %region_99.100_spmd, %region_100.101_spmd, %re... | conditional | bytes 1572960 | solution.py:43
  157.4 1.9 %collective-permute-start.233 = (f32[3,8,16,128]{3,2,1,0:T(8,128)S(1)}, f32[3,8,16,128]{3,2,1,0:T(8,128)}, u32[]{:S(2)}, u32[]{:S(2)}) collective-permute-start(f32[3,8,16,128]{3,2,1,0:T(8,128)S(1)} %param.116), channel_id=1, source_target_pairs={{0,320},{16,336},{32,352},{48,368},{64,384},{80,400},{96,416},{112... | collective-permute-start | bytes 589832 | tf_op jit(solution)/shard_map/cond/branch_20_fun/ppermute | solution.py:14
  159.3 6.3 %collective-permute-start.232 = (f32[3,8,16,128]{3,2,1,0:T(8,128)S(1)}, f32[3,8,16,128]{3,2,1,0:T(8,128)}, u32[]{:S(2)}, u32[]{:S(2)}) collective-permute-start(f32[3,8,16,128]{3,2,1,0:T(8,128)S(1)} %param.116), channel_id=1, source_target_pairs={{0,336},{16,352},{32,368},{48,384},{64,400},{80,416},{96,432},{112... | collective-permute-start | bytes 589832 | tf_op jit(solution)/shard_map/cond/branch_20_fun/ppermute | solution.py:14
  165.6 7.3 %collective-permute-done.233 = f32[3,8,16,128]{3,2,1,0:T(8,128)} collective-permute-done((f32[3,8,16,128]{3,2,1,0:T(8,128)S(1)}, f32[3,8,16,128]{3,2,1,0:T(8,128)}, u32[]{:S(2)}, u32[]{:S(2)}) %collective-permute-start.233) | collective-permute-done | bytes 196640 | tf_op jit(solution)/shard_map/cond/branch_20_fun/ppermute | solution.py:14
  172.9 10.0 %collective-permute-done.232 = f32[3,8,16,128]{3,2,1,0:T(8,128)} collective-permute-done((f32[3,8,16,128]{3,2,1,0:T(8,128)S(1)}, f32[3,8,16,128]{3,2,1,0:T(8,128)}, u32[]{:S(2)}, u32[]{:S(2)}) %collective-permute-start.232) | collective-permute-done | bytes 196640 | tf_op jit(solution)/shard_map/cond/branch_20_fun/ppermute | solution.py:14
  (59 shorter events, 23.4 us)
Async XLA Ops:
  4.0 0.7 copy-start.2
  5.9 21.4 %collective-permute-start.23 = (f32[3,8,16,128]{3,2,1,0:T(8,128)S(1)}, f32[3,8,16,128]{3,2,1,0:T(8,128)}, u32[]{:S(2)}, u32[]{:S(2)}) collective-permute-start(f32[3,8,16,128]{3,2,1,0:T(8,128)S(1)} %param.11), channel_id=1, source_target_pairs={{0,176},{16,192},{32,208},{48,224},{64,240},{80,256},{96,272},{112... | collective-permute-start | bytes 589832 | tf_op jit(solution)/shard_map/cond/branch_11_fun/ppermute | solution.py:14
  17.1 19.4 %collective-permute-start.22 = (f32[3,8,16,128]{3,2,1,0:T(8,128)S(1)}, f32[3,8,16,128]{3,2,1,0:T(8,128)}, u32[]{:S(2)}, u32[]{:S(2)}) collective-permute-start(f32[3,8,16,128]{3,2,1,0:T(8,128)S(1)} %param.11), channel_id=1, source_target_pairs={{0,192},{16,208},{32,224},{48,240},{64,256},{80,272},{96,288},{112... | collective-permute-start | bytes 589832 | tf_op jit(solution)/shard_map/cond/branch_11_fun/ppermute | solution.py:14
  37.8 13.8 %copy-start.1 = (s32[8,16,256]{2,1,0:T(8,128)S(1)}, s32[8,16,256]{2,1,0:T(8,128)}, u32[]{:S(2)}) copy-start(s32[8,16,256]{2,1,0:T(8,128)} %param.136) | copy-start | bytes 393220
  37.9 15.8 %collective-permute-start.259 = (f32[3,8,1,256]{3,2,1,0:T(1,128)S(1)}, f32[3,8,1,256]{3,2,1,0:T(1,128)S(1)}, u32[]{:S(2)}, u32[]{:S(2)}) collective-permute-start(f32[3,8,1,256]{3,2,1,0:T(1,128)S(1)} %get-tuple-element.166), channel_id=1, source_target_pairs={{0,1},{1,2},{2,3},{3,4},{4,5},{5,6},{6,7},{7,8},{8,9},{9,10},{10,1... | collective-permute-start | bytes 73736 | tf_op jit(solution)/shard_map/ppermute | solution.py:24
  42.6 11.1 %collective-permute-start.258 = (f32[3,8,1,256]{3,2,1,0:T(1,128)S(1)}, f32[3,8,1,256]{3,2,1,0:T(1,128)S(1)}, u32[]{:S(2)}, u32[]{:S(2)}) collective-permute-start(f32[3,8,1,256]{3,2,1,0:T(1,128)S(1)} %get-tuple-element.167), channel_id=1, source_target_pairs={{1,0},{2,1},{3,2},{4,3},{5,4},{6,5},{7,6},{8,7},{9,8},{10,9},{11,1... | collective-permute-start | bytes 73736 | tf_op jit(solution)/shard_map/ppermute | solution.py:27
  46.8 6.8 %collective-permute-start.257 = (f32[3,1,16,256]{3,2,1,0:T(8,128)S(1)}, f32[3,1,16,256]{3,2,1,0:T(8,128)S(1)}, u32[]{:S(2)}, u32[]{:S(2)}) collective-permute-start(f32[3,1,16,256]{3,2,1,0:T(8,128)S(1)} %get-tuple-element.164), channel_id=1, source_target_pairs={{0,16},{16,32},{32,48},{48,64},{64,80},{80,96},{96,112},{112,128},... | collective-permute-start | bytes 147464 | tf_op jit(solution)/shard_map/ppermute | solution.py:24
  48.8 5.7 %collective-permute-start.256 = (f32[3,1,16,256]{3,2,1,0:T(8,128)S(1)}, f32[3,1,16,256]{3,2,1,0:T(8,128)S(1)}, u32[]{:S(2)}, u32[]{:S(2)}) collective-permute-start(f32[3,1,16,256]{3,2,1,0:T(8,128)S(1)} %get-tuple-element.165), channel_id=1, source_target_pairs={{16,0},{32,16},{48,32},{64,48},{80,64},{96,80},{112,96},{128,112},... | collective-permute-start | bytes 147464 | tf_op jit(solution)/shard_map/ppermute | solution.py:27
  55.3 11.2 %collective-permute-start.103 = (f32[3,8,16,128]{3,2,1,0:T(8,128)S(1)}, f32[3,8,16,128]{3,2,1,0:T(8,128)}, u32[]{:S(2)}, u32[]{:S(2)}) collective-permute-start(f32[3,8,16,128]{3,2,1,0:T(8,128)S(1)} %param.51), channel_id=1, source_target_pairs={{0,304},{16,320},{32,336},{48,352},{64,368},{80,384},{96,400},{112... | collective-permute-start | bytes 589832 | tf_op jit(solution)/shard_map/cond/branch_19_fun/ppermute | solution.py:14
  58.3 20.5 %collective-permute-start.102 = (f32[3,8,16,128]{3,2,1,0:T(8,128)S(1)}, f32[3,8,16,128]{3,2,1,0:T(8,128)}, u32[]{:S(2)}, u32[]{:S(2)}) collective-permute-start(f32[3,8,16,128]{3,2,1,0:T(8,128)S(1)} %param.51), channel_id=1, source_target_pairs={{0,320},{16,336},{32,352},{48,368},{64,384},{80,400},{96,416},{112... | collective-permute-start | bytes 589832 | tf_op jit(solution)/shard_map/cond/branch_19_fun/ppermute | solution.py:14
  80.1 14.9 %collective-permute-start.261 = (f32[3,1,16,256]{3,2,1,0:T(8,128)S(1)}, f32[3,1,16,256]{3,2,1,0:T(8,128)S(1)}, u32[]{:S(2)}, u32[]{:S(2)}) collective-permute-start(f32[3,1,16,256]{3,2,1,0:T(8,128)S(1)} %get-tuple-element.158), channel_id=1, source_target_pairs={{0,16},{16,32},{32,48},{48,64},{64,80},{80,96},{96,112},{112,128},... | collective-permute-start | bytes 147464 | tf_op jit(solution)/shard_map/ppermute | solution.py:24
  82.1 13.0 %collective-permute-start.260 = (f32[3,1,16,256]{3,2,1,0:T(8,128)S(1)}, f32[3,1,16,256]{3,2,1,0:T(8,128)S(1)}, u32[]{:S(2)}, u32[]{:S(2)}) collective-permute-start(f32[3,1,16,256]{3,2,1,0:T(8,128)S(1)} %get-tuple-element.159), channel_id=1, source_target_pairs={{16,0},{32,16},{48,32},{64,48},{80,64},{96,80},{112,96},{128,112},... | collective-permute-start | bytes 147464 | tf_op jit(solution)/shard_map/ppermute | solution.py:27
  85.1 9.2 %collective-permute-start.263 = (f32[3,8,1,256]{3,2,1,0:T(1,128)S(1)}, f32[3,8,1,256]{3,2,1,0:T(1,128)S(1)}, u32[]{:S(2)}, u32[]{:S(2)}) collective-permute-start(f32[3,8,1,256]{3,2,1,0:T(1,128)S(1)} %get-tuple-element.160), channel_id=1, source_target_pairs={{0,1},{1,2},{2,3},{3,4},{4,5},{5,6},{6,7},{7,8},{8,9},{9,10},{10,1... | collective-permute-start | bytes 73736 | tf_op jit(solution)/shard_map/ppermute | solution.py:24
  87.5 8.0 %copy-start = (f32[3,8,16,256]{3,2,1,0:T(8,128)S(1)}, f32[3,8,16,256]{3,2,1,0:T(8,128)}, u32[]{:S(2)}) copy-start(f32[3,8,16,256]{3,2,1,0:T(8,128)} %param.134) | copy-start | bytes 1179652
  87.6 7.5 %collective-permute-start.262 = (f32[3,8,1,256]{3,2,1,0:T(1,128)S(1)}, f32[3,8,1,256]{3,2,1,0:T(1,128)S(1)}, u32[]{:S(2)}, u32[]{:S(2)}) collective-permute-start(f32[3,8,1,256]{3,2,1,0:T(1,128)S(1)} %get-tuple-element.161), channel_id=1, source_target_pairs={{1,0},{2,1},{3,2},{4,3},{5,4},{6,5},{7,6},{8,7},{9,8},{10,9},{11,1... | collective-permute-start | bytes 73736 | tf_op jit(solution)/shard_map/ppermute | solution.py:27
  96.7 24.6 %collective-permute-start.264 = (f32[3,1,16,256]{3,2,1,0:T(8,128)S(1)}, f32[3,1,16,256]{3,2,1,0:T(8,128)S(1)}, u32[]{:S(2)}, u32[]{:S(2)}) collective-permute-start(f32[3,1,16,256]{3,2,1,0:T(8,128)S(1)} %get-tuple-element.154), channel_id=1, source_target_pairs={{16,0},{32,16},{48,32},{64,48},{80,64},{96,80},{112,96},{128,112},... | collective-permute-start | bytes 147464 | tf_op jit(solution)/shard_map/ppermute | solution.py:27
  103.5 17.7 %collective-permute-start.265 = (f32[3,1,16,256]{3,2,1,0:T(8,128)S(1)}, f32[3,1,16,256]{3,2,1,0:T(8,128)S(1)}, u32[]{:S(2)}, u32[]{:S(2)}) collective-permute-start(f32[3,1,16,256]{3,2,1,0:T(8,128)S(1)} %get-tuple-element.155), channel_id=1, source_target_pairs={{0,16},{16,32},{32,48},{48,64},{64,80},{80,96},{96,112},{112,128},... | collective-permute-start | bytes 147464 | tf_op jit(solution)/shard_map/ppermute | solution.py:24
  105.5 10.2 %collective-permute-start.266 = (f32[3,8,1,256]{3,2,1,0:T(1,128)S(1)}, f32[3,8,1,256]{3,2,1,0:T(1,128)S(1)}, u32[]{:S(2)}, u32[]{:S(2)}) collective-permute-start(f32[3,8,1,256]{3,2,1,0:T(1,128)S(1)} %get-tuple-element.156), channel_id=1, source_target_pairs={{1,0},{2,1},{3,2},{4,3},{5,4},{6,5},{7,6},{8,7},{9,8},{10,9},{11,1... | collective-permute-start | bytes 73736 | tf_op jit(solution)/shard_map/ppermute | solution.py:27
  113.1 8.2 %collective-permute-start.267 = (f32[3,8,1,256]{3,2,1,0:T(1,128)S(1)}, f32[3,8,1,256]{3,2,1,0:T(1,128)S(1)}, u32[]{:S(2)}, u32[]{:S(2)}) collective-permute-start(f32[3,8,1,256]{3,2,1,0:T(1,128)S(1)} %get-tuple-element.157), channel_id=1, source_target_pairs={{0,1},{1,2},{2,3},{3,4},{4,5},{5,6},{6,7},{7,8},{8,9},{9,10},{10,1... | collective-permute-start | bytes 73736 | tf_op jit(solution)/shard_map/ppermute | solution.py:24
  122.0 10.1 %collective-permute-start.155 = (f32[3,8,16,128]{3,2,1,0:T(8,128)S(1)}, f32[3,8,16,128]{3,2,1,0:T(8,128)}, u32[]{:S(2)}, u32[]{:S(2)}) collective-permute-start(f32[3,8,16,128]{3,2,1,0:T(8,128)S(1)} %param.77), channel_id=1, source_target_pairs={{0,208},{16,224},{32,240},{48,256},{64,272},{80,288},{96,304},{112... | collective-permute-start | bytes 589832 | tf_op jit(solution)/shard_map/cond/branch_13_fun/ppermute | solution.py:14
  124.0 15.5 %collective-permute-start.154 = (f32[3,8,16,128]{3,2,1,0:T(8,128)S(1)}, f32[3,8,16,128]{3,2,1,0:T(8,128)}, u32[]{:S(2)}, u32[]{:S(2)}) collective-permute-start(f32[3,8,16,128]{3,2,1,0:T(8,128)S(1)} %param.77), channel_id=1, source_target_pairs={{0,224},{16,240},{32,256},{48,272},{64,288},{80,304},{96,320},{112... | collective-permute-start | bytes 589832 | tf_op jit(solution)/shard_map/cond/branch_13_fun/ppermute | solution.py:14
  140.6 16.1 %collective-permute-start.268 = (f32[3,1,16,256]{3,2,1,0:T(8,128)S(1)}, f32[3,1,16,256]{3,2,1,0:T(8,128)S(1)}, u32[]{:S(2)}, u32[]{:S(2)}) collective-permute-start(f32[3,1,16,256]{3,2,1,0:T(8,128)S(1)} %get-tuple-element.148), channel_id=1, source_target_pairs={{16,0},{32,16},{48,32},{64,48},{80,64},{96,80},{112,96},{128,112},... | collective-permute-start | bytes 147464 | tf_op jit(solution)/shard_map/ppermute | solution.py:27
  143.2 13.5 %collective-permute-start.269 = (f32[3,1,16,256]{3,2,1,0:T(8,128)S(1)}, f32[3,1,16,256]{3,2,1,0:T(8,128)S(1)}, u32[]{:S(2)}, u32[]{:S(2)}) collective-permute-start(f32[3,1,16,256]{3,2,1,0:T(8,128)S(1)} %get-tuple-element.149), channel_id=1, source_target_pairs={{0,16},{16,32},{32,48},{48,64},{64,80},{80,96},{96,112},{112,128},... | collective-permute-start | bytes 147464 | tf_op jit(solution)/shard_map/ppermute | solution.py:24
  146.2 7.5 %collective-permute-start.270 = (f32[3,8,1,256]{3,2,1,0:T(1,128)S(1)}, f32[3,8,1,256]{3,2,1,0:T(1,128)S(1)}, u32[]{:S(2)}, u32[]{:S(2)}) collective-permute-start(f32[3,8,1,256]{3,2,1,0:T(1,128)S(1)} %get-tuple-element.150), channel_id=1, source_target_pairs={{1,0},{2,1},{3,2},{4,3},{5,4},{6,5},{7,6},{8,7},{9,8},{10,9},{11,1... | collective-permute-start | bytes 73736 | tf_op jit(solution)/shard_map/ppermute | solution.py:27
  148.1 8.6 %collective-permute-start.271 = (f32[3,8,1,256]{3,2,1,0:T(1,128)S(1)}, f32[3,8,1,256]{3,2,1,0:T(1,128)S(1)}, u32[]{:S(2)}, u32[]{:S(2)}) collective-permute-start(f32[3,8,1,256]{3,2,1,0:T(1,128)S(1)} %get-tuple-element.151), channel_id=1, source_target_pairs={{0,1},{1,2},{2,3},{3,4},{4,5},{5,6},{6,7},{7,8},{8,9},{9,10},{10,1... | collective-permute-start | bytes 73736 | tf_op jit(solution)/shard_map/ppermute | solution.py:24
  157.4 15.5 %collective-permute-start.233 = (f32[3,8,16,128]{3,2,1,0:T(8,128)S(1)}, f32[3,8,16,128]{3,2,1,0:T(8,128)}, u32[]{:S(2)}, u32[]{:S(2)}) collective-permute-start(f32[3,8,16,128]{3,2,1,0:T(8,128)S(1)} %param.116), channel_id=1, source_target_pairs={{0,320},{16,336},{32,352},{48,368},{64,384},{80,400},{96,416},{112... | collective-permute-start | bytes 589832 | tf_op jit(solution)/shard_map/cond/branch_20_fun/ppermute | solution.py:14
  159.3 23.6 %collective-permute-start.232 = (f32[3,8,16,128]{3,2,1,0:T(8,128)S(1)}, f32[3,8,16,128]{3,2,1,0:T(8,128)}, u32[]{:S(2)}, u32[]{:S(2)}) collective-permute-start(f32[3,8,16,128]{3,2,1,0:T(8,128)S(1)} %param.116), channel_id=1, source_target_pairs={{0,336},{16,352},{32,368},{48,384},{64,400},{80,416},{96,432},{112... | collective-permute-start | bytes 589832 | tf_op jit(solution)/shard_map/cond/branch_20_fun/ppermute | solution.py:14
